TPU v7x, 128 devices: a whole 4x4x4 slice. The times are simulated.
128 devices in a mesh: tm: 4 (over x), mesh: 32 (over y, z, core).
Axes of the slice: x: 4, y: 4, z: 4, core: 2. Of those that a mesh axis runs over, the one named last changes fastest.
Arguments:
- right_sides: bfloat16 [8, 4096, 512], P('tm', 'mesh'), may hold values from -6 to 6
- diag_inverse: bfloat16 [8, 4096, 4096], P('tm', 'mesh'), may hold values from -0.09375 to 0.09375
- coupling: bfloat16 [8, 4096, 4096], P('tm', 'mesh'), may hold values from -0.0625 to 0.0625
- carry_in: bfloat16 [4096, 512], P('mesh'), may hold values from -6 to 6
- arrow_blocks: bfloat16 [8, 64, 4096], P('tm', None, 'mesh'), may hold values from -0.03125 to 0.03125
- tip_right: float32 [64, 512], replicated, may hold values from -6 to 6
- tip_inverse: float32 [64, 64], replicated, may hold values from -0.75 to 0.75
Outputs:
- forward_state: bfloat16 [8, 4096, 512], P('tm', 'mesh')
- tip_solution: float32 [64, 512], replicated
All inputs are finite; a program needn't handle non-finite values.
Results may differ from a plain program's by a relative error of at most 0.011.
Values may be sent and summed in bfloat16 or wider, within the bound.
A program may use at most 64 MiB of HBM per device.

v0:
```python
import jax
import jax.numpy as jnp
from jax import lax
from jax.sharding import PartitionSpec as P


def from_behind(block, axis, distance):
    devices = range(lax.axis_size(axis))
    route = [(i - distance, i) for i in devices if i - distance in devices]
    return lax.ppermute(block, axis, route)


def advance(matrix, source, earlier):
    coupled = jnp.dot(
        matrix,
        lax.all_gather(earlier, "mesh", axis=0, tiled=True),
        preferred_element_type=jnp.float32,
    )
    return (source - coupled).astype(jnp.bfloat16)


def body(right_sides, diag_inverse, coupling, carry_in, arrow_blocks, tip_right, tip_inverse):
    position = lax.axis_index("tm")
    devices_tm = lax.axis_size("tm")
    blocks, own_rows, columns = right_sides.shape
    scaled = jnp.einsum(
        "tij,tjr->tir",
        diag_inverse,
        lax.all_gather(right_sides, "mesh", axis=1, tiled=True),
        preferred_element_type=jnp.float32,
    )
    incoming = carry_in
    outputs = []
    for wave_step in range(devices_tm):
        current = incoming
        outputs = []
        for block_no in range(blocks):
            current = advance(coupling[block_no], scaled[block_no], current)
            outputs.append(current)
        if wave_step + 1 < devices_tm:
            moved = from_behind(current, "tm", 1)
            incoming = jnp.where(position == 0, carry_in, moved)
    solved = jnp.stack(outputs, axis=0)
    arrow_terms = jnp.einsum(
        "tfr,trs->fs", arrow_blocks, solved, preferred_element_type=jnp.float32
    )
    arrow_sum = lax.psum(arrow_terms, ("tm", "mesh"))
    tip_solution = jnp.dot(
        tip_inverse,
        tip_right - arrow_sum,
        precision=lax.Precision.HIGHEST,
        preferred_element_type=jnp.float32,
    )
    return (solved, tip_solution)


def solution(mesh):
    placed = (
        P("tm", "mesh", None),
        P("tm", "mesh", None),
        P("tm", "mesh", None),
        P("mesh", None),
        P("tm", None, "mesh"),
        P(),
        P(),
    )
    return jax.shard_map(
        body, mesh=mesh, in_specs=placed, out_specs=(P("tm", "mesh", None), P()), check_vma=False
    )
```

profile of v0, /device:TPU:1, one launch (start us, length us, event | category | flops | bytes accessed | tf_op | source)
XLA Modules:
  0.0 639.1 jit_solution(520782583988940051)
XLA Ops:
  7.2 0.7 all-gather.10.cloned.1.call-update
  8.0 0.7 all-gather.12.cloned.1.call-update
  8.7 58.4 %all-gather.10.cloned.1.call-done = bf16[2,4096,512]{2,1,0:T(8,128)(2,1)} async-done(((bf16[2,128,512]{2,1,0:T(8,128)(2,1)}), bf16[2,4096,512]{2,1,0:T(8,128)(2,1)}) %all-gather.10.cloned.1.call-update) | async-done | bytes 8388624 | tf_op jit(solution)/shard_map/all_gather | solution.py:29
  67.1 4.6 fusion.33
  71.8 43.6 %all-gather.12.cloned.1.call-done = bf16[4096,512]{1,0:T(8,128)(2,1)} async-done(((bf16[128,512]{1,0:T(8,128)(2,1)}), bf16[4096,512]{1,0:T(8,128)(2,1)}) %all-gather.12.cloned.1.call-update) | async-done | bytes 4194320 | tf_op jit(solution)/shard_map/all_gather | solution.py:16
  115.3 3.9 fusion.7
  119.3 45.8 %all-gather.14.cloned.1.call-done = bf16[4096,512]{1,0:T(8,128)(2,1)} async-done(((bf16[128,512]{1,0:T(8,128)(2,1)}), bf16[4096,512]{1,0:T(8,128)(2,1)}) %all-gather.14.cloned.1.call-update) | async-done | bytes 4194320 | tf_op jit(solution)/shard_map/all_gather | solution.py:16
  165.1 3.2 fusion.14
  168.3 3.1 collective-permute-start
  171.4 2.6 collective-permute-done
  174.0 0.7 broadcast_select_fusion.2
  174.8 47.6 %all-gather.16.cloned.1.call-done = bf16[4096,512]{1,0:T(8,128)(2,1)} async-done(((bf16[128,512]{1,0:T(8,128)(2,1)}), bf16[4096,512]{1,0:T(8,128)(2,1)}) %all-gather.16.cloned.1.call-update) | async-done | bytes 4194320 | tf_op jit(solution)/shard_map/all_gather | solution.py:16
  222.4 3.9 fusion.13
  226.4 45.8 %all-gather.18.cloned.1.call-done = bf16[4096,512]{1,0:T(8,128)(2,1)} async-done(((bf16[128,512]{1,0:T(8,128)(2,1)}), bf16[4096,512]{1,0:T(8,128)(2,1)}) %all-gather.18.cloned.1.call-update) | async-done | bytes 4194320 | tf_op jit(solution)/shard_map/all_gather | solution.py:16
  272.2 3.2 fusion.12
  275.4 3.1 collective-permute-start.1
  278.5 2.6 collective-permute-done.1
  281.1 0.7 broadcast_select_fusion.1
  281.9 47.6 %all-gather.20.cloned.1.call-done = bf16[4096,512]{1,0:T(8,128)(2,1)} async-done(((bf16[128,512]{1,0:T(8,128)(2,1)}), bf16[4096,512]{1,0:T(8,128)(2,1)}) %all-gather.20.cloned.1.call-update) | async-done | bytes 4194320 | tf_op jit(solution)/shard_map/all_gather | solution.py:16
  329.5 3.9 fusion.11
  333.4 45.8 %all-gather.22.cloned.1.call-done = bf16[4096,512]{1,0:T(8,128)(2,1)} async-done(((bf16[128,512]{1,0:T(8,128)(2,1)}), bf16[4096,512]{1,0:T(8,128)(2,1)}) %all-gather.22.cloned.1.call-update) | async-done | bytes 4194320 | tf_op jit(solution)/shard_map/all_gather | solution.py:16
  379.2 3.2 fusion.10
  382.5 3.1 collective-permute-start.2
  385.6 2.6 collective-permute-done.2
  388.2 0.7 broadcast_select_fusion
  389.0 47.6 %all-gather.24.cloned.1.call-done = bf16[4096,512]{1,0:T(8,128)(2,1)} async-done(((bf16[128,512]{1,0:T(8,128)(2,1)}), bf16[4096,512]{1,0:T(8,128)(2,1)}) %all-gather.24.cloned.1.call-update) | async-done | bytes 4194320 | tf_op jit(solution)/shard_map/all_gather | solution.py:16
  436.6 3.9 fusion.9
  440.6 45.8 %all-gather.26.cloned.1.call-done = bf16[4096,512]{1,0:T(8,128)(2,1)} async-done(((bf16[128,512]{1,0:T(8,128)(2,1)}), bf16[4096,512]{1,0:T(8,128)(2,1)}) %all-gather.26.cloned.1.call-update) | async-done | bytes 4194320 | tf_op jit(solution)/shard_map/all_gather | solution.py:16
  486.4 3.2 fusion.15
  489.7 0.8 convolution_bitcast_fusion.7
  490.5 139.9 %all-reduce.2.cloned.1.call-done = f32[64,512]{1,0:T(8,128)} async-done(((f32[64,512]{1,0:T(8,128)}), f32[64,512]{1,0:T(8,128)}) %all-reduce.2.cloned.1.call-update) | async-done | bytes 131088 | tf_op jit(solution)/shard_map/psum | solution.py:47
  630.4 1.8 convolution_bitcast_fusion.8
  (33 shorter events, 0.6 us)
Async XLA Ops:
  7.2 60.0 %copy-start = (bf16[2,128,4096]{2,1,0:T(8,128)(2,1)S(1)}, bf16[2,128,4096]{2,1,0:T(8,128)(2,1)}, u32[]{:S(2)}) copy-start(bf16[2,128,4096]{2,1,0:T(8,128)(2,1)} %param.8) | copy-start | bytes 6291460
  7.2 59.9 %all-gather.10.cloned.1.call-start = ((), (), s32[]{:S(2)}) async-start(), calls=%async_computation | async-start | bytes 8650752 | tf_op jit(solution)/shard_map/all_gather | solution.py:29
  7.9 107.4 %all-gather.12.cloned.1.call-start = ((), (), s32[]{:S(2)}) async-start(), calls=%async_computation.1 | async-start | bytes 4325376 | tf_op jit(solution)/shard_map/all_gather | solution.py:16
  8.7 156.4 %all-gather.14.cloned.1.call-start = ((), (), s32[]{:S(2)}) async-start(), calls=%async_computation.2 | async-start | bytes 4325376 | tf_op jit(solution)/shard_map/all_gather | solution.py:16
  119.2 54.8 %copy-start.1 = (bf16[128,512]{1,0:T(8,128)(2,1)S(1)}, bf16[128,512]{1,0:T(8,128)(2,1)}, u32[]{:S(2)}) copy-start(bf16[128,512]{1,0:T(8,128)(2,1)} %param.10) | copy-start | bytes 393220
  119.2 103.2 %all-gather.16.cloned.1.call-start = ((), (), s32[]{:S(2)}) async-start(), calls=%async_computation.3 | async-start | bytes 4325376 | tf_op jit(solution)/shard_map/all_gather | solution.py:16
  168.3 5.7 collective-permute-start
  174.7 97.4 %all-gather.18.cloned.1.call-start = ((), (), s32[]{:S(2)}) async-start(), calls=%async_computation.4 | async-start | bytes 4325376 | tf_op jit(solution)/shard_map/all_gather | solution.py:16
  226.3 103.2 %all-gather.20.cloned.1.call-start = ((), (), s32[]{:S(2)}) async-start(), calls=%async_computation.5 | async-start | bytes 4325376 | tf_op jit(solution)/shard_map/all_gather | solution.py:16
  275.4 5.7 collective-permute-start.1
  281.8 97.4 %all-gather.22.cloned.1.call-start = ((), (), s32[]{:S(2)}) async-start(), calls=%async_computation.6 | async-start | bytes 4325376 | tf_op jit(solution)/shard_map/all_gather | solution.py:16
  333.4 103.2 %all-gather.24.cloned.1.call-start = ((), (), s32[]{:S(2)}) async-start(), calls=%async_computation.7 | async-start | bytes 4325376 | tf_op jit(solution)/shard_map/all_gather | solution.py:16
  382.5 5.7 collective-permute-start.2
  388.9 97.4 %all-gather.26.cloned.1.call-start = ((), (), s32[]{:S(2)}) async-start(), calls=%async_computation.8 | async-start | bytes 4325376 | tf_op jit(solution)/shard_map/all_gather | solution.py:16
  440.5 49.1 %copy-start.2 = (bf16[128,512]{1,0:T(8,128)(2,1)S(1)}, bf16[128,512]{1,0:T(8,128)(2,1)}, u32[]{:S(2)}) copy-start(bf16[128,512]{1,0:T(8,128)(2,1)} %fusion.9) | copy-start | bytes 393220
  440.5 49.2 %copy-start.5 = (bf16[2,64,128]{2,1,0:T(8,128)(2,1)S(1)}, bf16[2,64,128]{2,1,0:T(8,128)(2,1)}, u32[]{:S(2)}) copy-start(bf16[2,64,128]{2,1,0:T(8,128)(2,1)} %param.11) | copy-start | bytes 98308
  440.5 189.9 %copy-start.4 = (f32[64,512]{1,0:T(8,128)S(1)}, f32[64,512]{1,0:T(8,128)}, u32[]{:S(2)}) copy-start(f32[64,512]{1,0:T(8,128)} %param.12) | copy-start | bytes 393220
  440.5 189.9 %copy-start.6 = (f32[64,64]{1,0:T(8,128)S(1)}, f32[64,64]{1,0:T(8,128)}, u32[]{:S(2)}) copy-start(f32[64,64]{1,0:T(8,128)} %param.13) | copy-start | bytes 49156
  440.5 189.9 %all-reduce.2.cloned.1.call-start = ((), (), s32[]{:S(2)}) async-start(), calls=%async_computation.9 | async-start | bytes 262144 | tf_op jit(solution)/shard_map/psum | solution.py:47
  489.6 142.6 %copy-start.3 = (bf16[2,128,512]{2,1,0:T(8,128)(2,1)}, bf16[2,128,512]{2,1,0:T(8,128)(2,1)S(1)}, u32[]{:S(2)}) copy-start(bf16[2,128,512]{2,1,0:T(8,128)(2,1)S(1)} %pad_maximum_fusion) | copy-start | bytes 786436
Sparse Core Ops, SparseCore 0:
  10.4 56.6 all-gather.9
  69.4 45.8 all-gather.11
  119.4 45.6 all-gather.13
  174.8 47.5 all-gather.15
  226.4 45.6 all-gather.17
  281.9 47.4 all-gather.19
  333.5 45.6 all-gather.21
  389.0 47.5 all-gather.23
  440.6 45.6 all-gather.25
  491.5 138.8 all-reduce.1
where the time goes:
time: 639 us
  waiting for transfers between devices  577 us (90%)
  matrix products  35.8 us (6%)
  between operations  14.3 us (2%)
  starting transfers between devices  9.72 us (2%)
    all_gather x8, waiting for transfers between devices, advance(): lax.all_gather(earlier, 'mesh', axis=0, tiled=True)  370 us
    psum x1, waiting for transfers between devices, body(): arrow_sum = lax.psum(arrow_terms, ('tm', 'mesh'))  140 us
    all_gather x1, waiting for transfers between devices, body(): lax.all_gather(right_sides, 'mesh', axis=1, tiled=True)  58.4 us
    dot_general x8, matrix products, advance(): jnp.dot(matrix, lax.all_gather(earlier, 'mesh', axis=0, tiled=True), pref...  28.5 us
  transfers between devices with their start and end apart: 13, of which 13 were waited for; matrix products, arithmetic and copies ran while one was open for 1% of the time, Pallas kernels for 0%

commit v1 on v0

--- a/solution.py
+++ b/solution.py
@@ -2,6 +2,13 @@
 import jax.numpy as jnp
 from jax import lax
 from jax.sharding import PartitionSpec as P
+
+
+def exchange_gather(x, name, along):
+    peers = lax.axis_size(name)
+    blocks = jnp.stack([x for _ in range(peers)])
+    blocks = lax.all_to_all(blocks, name, split_axis=0, concat_axis=0)
+    return jnp.concatenate(blocks, axis=along)
 
 
 def from_behind(block, axis, distance):
@@ -12,9 +19,7 @@
 
 def advance(matrix, source, earlier):
     coupled = jnp.dot(
-        matrix,
-        lax.all_gather(earlier, "mesh", axis=0, tiled=True),
-        preferred_element_type=jnp.float32,
+        matrix, exchange_gather(earlier, "mesh", 0), preferred_element_type=jnp.float32
     )
     return (source - coupled).astype(jnp.bfloat16)
 

time: 639 us -> 672 us (1.052)
  blocking collectives: 0 us -> 384 us
  waiting for transfers between devices: 577 us -> 229 us
  matrix products: 35.8 us -> 15.9 us
  starting transfers between devices: 9.72 us -> 21 us
    all_to_all x0 -> x7, blocking collectives: none -> 384 us  [exchange_gather(): blocks = lax.all_to_all(blocks, name, split_axis=0, concat_axis=0)]
    all_gather x8 -> x0, waiting for transfers between devices: 370 us -> none  [advance(): lax.all_gather(earlier, 'mesh', axis=0, tiled=True)]
    all_gather x1, waiting for transfers between devices: 58.4 us -> 81.3 us  [body(): lax.all_gather(right_sides, 'mesh', axis=1, tiled=True)]
    dot_general x8, matrix products: 28.5 us -> 8.63 us  [advance(): jnp.dot(matrix, exchange_gather(earlier, 'mesh', 0), preferred_element_ty...]
    all_to_all x0 -> x1, starting transfers between devices: none -> 9.66 us  [exchange_gather(): blocks = lax.all_to_all(blocks, name, split_axis=0, concat_axis=0)]
  transfers between devices with their start and end apart: 13 -> 6, of which waited for: 13 -> 5; matrix products, arithmetic and copies ran while one was open for 1% -> 1% of each run, Pallas kernels for 0% -> 0%
where the time goes in v1:
time: 672 us; the launch traced here: 671 us
  blocking collectives  384 us (57%)
  waiting for transfers between devices  229 us (34%)
  starting transfers between devices  21 us (3%)
  matrix products  15.9 us (2%)
  between operations  14.3 us (2%)
    all_to_all x7, blocking collectives, exchange_gather(): blocks = lax.all_to_all(blocks, name, split_axis=0, concat_axis=0)  384 us
    psum x1, waiting for transfers between devices, body(): arrow_sum = lax.psum(arrow_terms, ('tm', 'mesh'))  139 us
    all_gather x1, waiting for transfers between devices, body(): lax.all_gather(right_sides, 'mesh', axis=1, tiled=True)  81.3 us
  transfers between devices with their start and end apart: 6, of which 5 were waited for; matrix products, arithmetic and copies ran while one was open for 1% of the time, Pallas kernels for 0%

profile of v1, /device:TPU:1, one launch (start us, length us, event | category | flops | bytes accessed | tf_op | source)
XLA Modules:
  0.0 671.0 jit_solution(13531949215109856053)
XLA Ops:
  7.2 0.7 all-gather.2.cloned.1.call-update
  7.9 3.3 stack.22
  11.2 9.7 %all-to-all-start = ((bf16[32,128,512]{2,1,0:T(8,128)(2,1)}), bf16[32,128,512]{2,1,0:T(8,128)(2,1)}, u32[]{:S(2)}, u32[]{:S(2)}) async-start(bf16[32,128,512]{2,1,0:T(8,128)(2,1)} %stack.22), calls=%async_computation | async-start | bytes 8388608 | tf_op jit(solution)/shard_map/all_to_all | solution.py:10
  20.9 81.3 %all-gather.2.cloned.1.call-done = bf16[2,4096,512]{2,1,0:T(8,128)(2,1)} async-done(((bf16[2,128,512]{2,1,0:T(8,128)(2,1)}), bf16[2,4096,512]{2,1,0:T(8,128)(2,1)}) %all-gather.2.cloned.1.call-update) | async-done | bytes 8388624 | tf_op jit(solution)/shard_map/all_gather | solution.py:34
  102.3 4.6 fusion.33
  106.9 3.2 fusion.7
  110.2 0.5 stack.23
  110.6 56.0 %all_to_all.40 = bf16[32,128,512]{2,1,0:T(8,128)(2,1)S(1)} all-to-all(bf16[32,128,512]{2,1,0:T(8,128)(2,1)S(1)} %stack.23), channel_id=1, replica_groups=mesh['tm'=4,'mesh'=32] {'mesh'}, dimensions={0} | all-to-all | bytes 8388608 | tf_op jit(solution)/shard_map/all_to_all | solution.py:10
  166.7 0.8 fusion.14
  167.5 3.1 collective-permute-start
  170.6 2.7 collective-permute-done
  173.8 54.9 %all_to_all.41 = bf16[32,128,512]{2,1,0:T(8,128)(2,1)S(1)} all-to-all(bf16[32,128,512]{2,1,0:T(8,128)(2,1)S(1)} %stack.24), channel_id=1, replica_groups=mesh['tm'=4,'mesh'=32] {'mesh'}, dimensions={0} | all-to-all | bytes 8388608 | tf_op jit(solution)/shard_map/all_to_all | solution.py:10
  228.7 0.8 fusion.13
  229.5 0.5 stack.25
  230.0 54.4 %all_to_all.42 = bf16[32,128,512]{2,1,0:T(8,128)(2,1)S(1)} all-to-all(bf16[32,128,512]{2,1,0:T(8,128)(2,1)S(1)} %stack.25), channel_id=1, replica_groups=mesh['tm'=4,'mesh'=32] {'mesh'}, dimensions={0} | all-to-all | bytes 8388608 | tf_op jit(solution)/shard_map/all_to_all | solution.py:10
  284.3 0.8 fusion.12
  285.1 4.1 collective-permute-start.1
  289.2 2.7 collective-permute-done.1
  292.0 0.5 stack.26
  292.5 54.9 %all_to_all.43 = bf16[32,128,512]{2,1,0:T(8,128)(2,1)S(1)} all-to-all(bf16[32,128,512]{2,1,0:T(8,128)(2,1)S(1)} %stack.26), channel_id=1, replica_groups=mesh['tm'=4,'mesh'=32] {'mesh'}, dimensions={0} | all-to-all | bytes 8388608 | tf_op jit(solution)/shard_map/all_to_all | solution.py:10
  347.3 0.8 fusion.11
  348.6 54.4 %all_to_all.44 = bf16[32,128,512]{2,1,0:T(8,128)(2,1)S(1)} all-to-all(bf16[32,128,512]{2,1,0:T(8,128)(2,1)S(1)} %stack.27), channel_id=1, replica_groups=mesh['tm'=4,'mesh'=32] {'mesh'}, dimensions={0} | all-to-all | bytes 8388608 | tf_op jit(solution)/shard_map/all_to_all | solution.py:10
  403.0 0.8 fusion.10
  403.8 4.1 collective-permute-start.2
  407.9 2.7 collective-permute-done.2
  411.1 54.9 %all_to_all.45 = bf16[32,128,512]{2,1,0:T(8,128)(2,1)S(1)} all-to-all(bf16[32,128,512]{2,1,0:T(8,128)(2,1)S(1)} %stack.28), channel_id=1, replica_groups=mesh['tm'=4,'mesh'=32] {'mesh'}, dimensions={0} | all-to-all | bytes 8388608 | tf_op jit(solution)/shard_map/all_to_all | solution.py:10
  466.0 0.8 fusion.9
  467.3 54.6 %all_to_all.46 = bf16[32,128,512]{2,1,0:T(8,128)(2,1)S(1)} all-to-all(bf16[32,128,512]{2,1,0:T(8,128)(2,1)S(1)} %stack.30), channel_id=1, replica_groups=mesh['tm'=4,'mesh'=32] {'mesh'}, dimensions={0} | all-to-all | bytes 8388608 | tf_op jit(solution)/shard_map/all_to_all | solution.py:10
  521.9 0.7 fusion.15
  522.7 0.8 convolution_bitcast_fusion.7
  523.5 138.8 %all-reduce.2.cloned.1.call-done = f32[64,512]{1,0:T(8,128)} async-done(((f32[64,512]{1,0:T(8,128)}), f32[64,512]{1,0:T(8,128)}) %all-reduce.2.cloned.1.call-update) | async-done | bytes 131088 | tf_op jit(solution)/shard_map/psum | solution.py:52
  662.3 1.8 convolution_bitcast_fusion.8
  (30 shorter events, 2.1 us)
Async XLA Ops:
  7.2 95.1 %copy-start = (bf16[2,128,4096]{2,1,0:T(8,128)(2,1)S(1)}, bf16[2,128,4096]{2,1,0:T(8,128)(2,1)}, u32[]{:S(2)}) copy-start(bf16[2,128,4096]{2,1,0:T(8,128)(2,1)} %param.8) | copy-start | bytes 6291460
  7.2 95.1 %all-gather.2.cloned.1.call-start = ((), (), s32[]{:S(2)}) async-start(), calls=%async_computation.8 | async-start | bytes 8650752 | tf_op jit(solution)/shard_map/all_gather | solution.py:34
  11.2 95.7 %all-to-all-start = ((bf16[32,128,512]{2,1,0:T(8,128)(2,1)}), bf16[32,128,512]{2,1,0:T(8,128)(2,1)}, u32[]{:S(2)}, u32[]{:S(2)}) async-start(bf16[32,128,512]{2,1,0:T(8,128)(2,1)} %stack.22), calls=%async_computation | async-start | bytes 8388608 | tf_op jit(solution)/shard_map/all_to_all | solution.py:10
  20.9 641.4 %all-reduce.2.cloned.1.call-start = ((), (), s32[]{:S(2)}) async-start(), calls=%async_computation.9 | async-start | bytes 262144 | tf_op jit(solution)/shard_map/psum | solution.py:52
  110.6 56.1 %copy-start.2 = (bf16[2,128,4096]{2,1,0:T(8,128)(2,1)S(1)}, bf16[2,128,4096]{2,1,0:T(8,128)(2,1)}, u32[]{:S(2)}) copy-start(bf16[2,128,4096]{2,1,0:T(8,128)(2,1)} %param.9) | copy-start | bytes 6291460
  166.7 6.6 copy-start.4
  167.5 5.9 collective-permute-start
  285.1 6.8 %collective-permute-start.1 = (bf16[128,512]{1,0:T(8,128)(2,1)S(1)}, bf16[128,512]{1,0:T(8,128)(2,1)S(1)}, u32[]{:S(2)}, u32[]{:S(2)}) collective-permute-start(bf16[128,512]{1,0:T(8,128)(2,1)S(1)} %fusion.12), channel_id=1, source_target_pairs={{0,32},{32,64},{64,96},{1,33},{33,65},{65,97},{2,34},{34,66},{66,9... | collective-permute-start | bytes 393224 | tf_op jit(solution)/shard_map/ppermute | solution.py:17
  403.8 6.8 %collective-permute-start.2 = (bf16[128,512]{1,0:T(8,128)(2,1)S(1)}, bf16[128,512]{1,0:T(8,128)(2,1)S(1)}, u32[]{:S(2)}, u32[]{:S(2)}) collective-permute-start(bf16[128,512]{1,0:T(8,128)(2,1)S(1)} %fusion.10), channel_id=1, source_target_pairs={{0,32},{32,64},{64,96},{1,33},{33,65},{65,97},{2,34},{34,66},{66,9... | collective-permute-start | bytes 393224 | tf_op jit(solution)/shard_map/ppermute | solution.py:17
  467.2 54.7 %copy-start.3 = (bf16[2,128,4096]{2,1,0:T(8,128)(2,1)S(1)}, bf16[2,128,4096]{2,1,0:T(8,128)(2,1)}, u32[]{:S(2)}) copy-start(bf16[2,128,4096]{2,1,0:T(8,128)(2,1)} %param.9) | copy-start | bytes 6291460
  467.2 196.9 %copy-start.1 = (bf16[2,128,4096]{2,1,0:T(8,128)(2,1)S(1)}, bf16[2,128,4096]{2,1,0:T(8,128)(2,1)}, u32[]{:S(2)}) copy-start(bf16[2,128,4096]{2,1,0:T(8,128)(2,1)} %param.8) | copy-start | bytes 6291460
  521.9 0.8 copy-start.7
  521.9 140.4 %copy-start.6 = (f32[64,512]{1,0:T(8,128)S(1)}, f32[64,512]{1,0:T(8,128)}, u32[]{:S(2)}) copy-start(f32[64,512]{1,0:T(8,128)} %param.12) | copy-start | bytes 393220
  521.9 140.4 %copy-start.8 = (f32[64,64]{1,0:T(8,128)S(1)}, f32[64,64]{1,0:T(8,128)}, u32[]{:S(2)}) copy-start(f32[64,64]{1,0:T(8,128)} %param.13) | copy-start | bytes 49156
  522.7 141.5 %copy-start.5 = (bf16[2,128,512]{2,1,0:T(8,128)(2,1)}, bf16[2,128,512]{2,1,0:T(8,128)(2,1)S(1)}, u32[]{:S(2)}) copy-start(bf16[2,128,512]{2,1,0:T(8,128)(2,1)S(1)} %pad_maximum_fusion) | copy-start | bytes 786436
Sparse Core Ops, SparseCore 0:
  10.4 91.8 all-gather.1
  523.7 138.5 all-reduce.1
